TPU v7x, 128 devices: a whole 4x4x4 slice. The times are simulated.
128 devices in a mesh: ex: 16 (over y, x), lay: 8 (over z, core).
Axes of the slice: x: 4, y: 4, z: 4, core: 2. Of those that a mesh axis runs over, the one named last changes fastest.
Arguments:
- grads: bfloat16 [8, 16384, 4096], P('lay', 'ex'), may hold values from -0.119628906 to 0.119628906
- prec_in: bfloat16 [8, 64, 64], P('lay'), as said below
- prec_out: bfloat16 [8, 64, 64], P('lay'), as said below
- requests: int32 [16, 16], replicated, may hold values from 0 to 7
- pairs: int32 [1024, 2], P('ex'), may hold values from 0 to 127, as said below
Outputs:
- gram: float32 [1024, 128, 128], P(('ex', 'lay'))
Inputs may be any that keep to these rules, and one draw needn't show every extreme that they name: Each device's listed first blocks are its own: pairs[p, 0] lies in 8 * (p // 64) to 8 * (p // 64 + 1) - 1. pairs[p, 1] is a device number of ex. The 64 pairs of one device are distinct and name every device number at least once. `prec_in`: each matrix has a diagonal between 1.5 and 6 and exceeds the sum of magnitudes of the rest of its row. `prec_out`: each matrix has a diagonal between 1.5 and 6 and exceeds the sum of magnitudes of the rest of its row.
All inputs are finite; a program needn't handle non-finite values.
Results may differ from a plain program's by a relative error of at most 0.0026.
Values may be sent and summed in bfloat16 or wider, within the bound.
No kernel may reach another device: no remote copies, remote signals or barrier semaphores. Data moves between devices by JAX's collectives and lax.ppermute only.
A program may use at most 128 MiB of HBM per device.

v0:
```python
import jax
import jax.numpy as jnp
from jax import lax
from jax.sharding import PartitionSpec as P

BLOCK = 128


def precondition(grads, prec_in, prec_out):
    layer_count, example_rows, width = grads.shape
    rank = prec_in.shape[-1]
    turned = jnp.swapaxes(grads, 1, 2).reshape(layer_count, rank, rank, example_rows)
    inner = jnp.einsum(
        "loie,lij->loje", turned, prec_in, preferred_element_type=jnp.float32
    ).astype(jnp.bfloat16)
    outer = jnp.einsum("lpo,loje->lpje", prec_out, inner, preferred_element_type=jnp.float32)
    return outer.astype(jnp.bfloat16).reshape(layer_count, width, example_rows)


def pick_tiles(products, first, source):
    return products[first, :, source, :]


def on_device(grads, prec_in, prec_out, requests, pairs):
    layer_count, example_rows, width = grads.shape
    blocks = grads.reshape(layer_count, example_rows // BLOCK, BLOCK, width)
    block_count = blocks.shape[1]
    member = lax.axis_index("ex")
    wanted = lax.dynamic_index_in_dim(requests, member, axis=1, keepdims=False)
    outgoing = jnp.take(blocks, wanted, axis=1)
    incoming = lax.all_to_all(outgoing, "ex", split_axis=1, concat_axis=1, tiled=True)
    holders = incoming.shape[1]
    left = precondition(grads, prec_in, prec_out)
    right = incoming.reshape(layer_count, holders * BLOCK, width)
    products = jnp.einsum("lqx,lmq->xm", left, right, preferred_element_type=jnp.float32)
    products = products.reshape(block_count, BLOCK, holders, BLOCK)
    first = pairs[:, 0] - member * block_count
    source = pairs[:, 1]
    pair_count = pairs.shape[0]
    share = pair_count // lax.axis_size("lay")
    terms = pick_tiles(products, first, source)
    total = lax.psum(terms, "lay")
    return lax.dynamic_slice_in_dim(total, lax.axis_index("lay") * share, share, 0)


def solution(mesh):
    placed = (P("lay", "ex", None), P("lay", None, None), P("lay", None, None), P(), P("ex", None))
    return jax.shard_map(
        on_device,
        mesh=mesh,
        in_specs=placed,
        out_specs=P(("ex", "lay"), None, None),
        check_vma=False,
    )
```

profile of v0, /device:TPU:0, one launch (start us, length us, event | category | flops | bytes accessed | tf_op | source)
XLA Modules:
  0.0 400.7 jit_solution(12002217262961592764)
XLA Ops:
  6.5 0.0 copy-start
  6.5 0.9 fusion.8
  7.4 0.9 and_reduce_fusion
  8.3 10.5 %gather_fusion = bf16[16,128,4096]{2,1,0:T(8,128)(2,1)} fusion(bf16[8,128,4096]{2,1,0:T(8,128)(2,1)} %bitcast.39, s32[1024]{0:T(1024)S(1)} %pad_clamp_fusion), kind=kCustom, calls=%fused_computation | custom fusion | bytes 33554496 | tf_op jit(solution)/shard_map/jit(_take)/gather | solution.py:30
  18.8 14.2 %bitcast_select_fusion = bf16[1,16,128,4096]{3,2,0,1:T(8,128)(2,1)} fusion(bf16[16,128,4096]{2,1,0:T(8,128)(2,1)} %gather_fusion, pred[16]{0:T(512)(128)(4,1)S(1)} %and_reduce_fusion), kind=kLoop, calls=%fused_computation.4 | loop fusion | flops 8388608 | bytes 33554448 | tf_op jit(solution)/shard_map/jit(_take)/select_n | solution.py:30
  33.0 7.2 %all-to-all-start = ((bf16[1,16,128,4096]{3,2,0,1:T(8,128)(2,1)}), bf16[1,16,128,4096]{3,2,0,1:T(8,128)(2,1)}, u32[]{:S(2)}, u32[]{:S(2)}) async-start(bf16[1,16,128,4096]{3,2,0,1:T(8,128)(2,1)} %bitcast_select_fusion), calls=%async_computation | async-start | bytes 33554432 | tf_op jit(solution)/shard_map/all_to_all | solution.py:31
  40.2 0.0 all-reduce.2.cloned.1.call-start
  40.3 12.0 %copy.14 = bf16[1,1024,4096]{1,2,0:T(8,128)(2,1)} copy(bf16[1,1024,4096]{2,1,0:T(8,128)(2,1)} %param.5) | data formatting | bytes 16777216 | tf_op args[0]
  52.2 0.0 copy-done
  52.2 0.0 copy-start.2
  52.2 5.8 %convert_bitcast_fusion.1 = bf16[64,64,1024]{2,1,0:T(8,128)(2,1)S(1)} fusion(bf16[64,64,1024]{2,1,0:T(8,128)(2,1)} %bitcast.40, bf16[1,64,64]{2,1,0:T(8,128)(2,1)S(1)} %copy-done), kind=kOutput, calls=%fused_computation.8 | convolution fusion | flops 541065216 | bytes 16785408 | tf_op jit(solution)/shard_map/loie,lij->loje/dot_general | solution.py:13
  58.0 0.0 copy-done.2
  58.0 12.9 %convert_bitcast_fusion = bf16[64,64,1024]{2,0,1:T(8,128)(2,1)} fusion(bf16[64,64,1024]{2,1,0:T(8,128)(2,1)S(1)} %convert_bitcast_fusion.1, bf16[1,64,64]{2,1,0:T(8,128)(2,1)S(1)} %copy-done.2), kind=kOutput, calls=%fused_computation.7 | convolution fusion | flops 541065216 | bytes 16785408 | tf_op jit(solution)/shard_map/lpo,loje->lpje/dot_general | solution.py:16
  70.9 11.3 %copy.17 = bf16[64,64,1024]{2,1,0:T(8,128)(2,1)} copy(bf16[64,64,1024]{2,0,1:T(8,128)(2,1)} %convert_bitcast_fusion) | data formatting | bytes 16777216 | tf_op jit(solution)/shard_map/convert_element_type | solution.py:17
  82.2 0.0 copy-start.3
  82.2 11.2 %copy.22 = bf16[1024,4096]{1,0:T(8,128)(2,1)} copy(bf16[1024,4096]{0,1:T(8,128)(2,1)} %bitcast.41) | data formatting | bytes 16777216 | tf_op jit(solution)/shard_map/lqx,lmq->xm/dot_general | solution.py:35
  93.4 0.0 copy-done.3
  93.4 196.5 %all-to-all-done = bf16[1,16,128,4096]{3,2,0,1:T(8,128)(2,1)} async-done(((bf16[1,16,128,4096]{3,2,0,1:T(8,128)(2,1)}), bf16[1,16,128,4096]{3,2,0,1:T(8,128)(2,1)}, u32[]{:S(2)}, u32[]{:S(2)}) %all-to-all-start) | async-done | bytes 16777248 | tf_op jit(solution)/shard_map/all_to_all | solution.py:31
  289.9 0.0 copy-start.1
  289.9 24.1 %fusion = f32[8,128,16,128]{3,1,2,0:T(8,128)} fusion(bf16[8,128,4096,1]{2,1,3,0:T(8,128)(2,1)} %bitcast.42, bf16[1,16,128,4096]{3,2,0,1:T(8,128)(2,1)} %all-to-all-done), kind=kOutput, calls=%fused_computation.2 | convolution fusion | flops 17179869184 | bytes 33554432 | tf_op jit(solution)/shard_map/lqx,lmq->xm/dot_general | solution.py:35
  314.0 6.1 %gather_fusion.1 = f32[64,128,128]{2,1,0:T(8,128)} fusion(f32[8,128,16,128]{3,1,2,0:T(8,128)} %fusion, s32[64]{0:T(128)S(1)} %fusion.14), kind=kCustom, calls=%fused_computation.1 | custom fusion | bytes 8389120 | tf_op jit(solution)/shard_map/gather | solution.py:21
  320.2 0.0 all-reduce.2.cloned.1.call-update
  320.2 71.8 %all-reduce.2.cloned.1.call-done = f32[64,128,128]{2,1,0:T(8,128)} async-done(((f32[64,128,128]{2,1,0:T(8,128)}), f32[64,128,128]{2,1,0:T(8,128)}) %all-reduce.2.cloned.1.call-update) | async-done | bytes 4194320 | tf_op jit(solution)/shard_map/psum | solution.py:42
  392.0 1.9 constant_dynamic-slice_fusion
  393.9 0.0 copy-done.1
  (2 shorter events, 0.0 us)
Async XLA Ops:
  6.5 45.7 %copy-start = (bf16[1,64,64]{2,1,0:T(8,128)(2,1)S(1)}, bf16[1,64,64]{2,1,0:T(8,128)(2,1)}, u32[]{:S(2)}) copy-start(bf16[1,64,64]{2,1,0:T(8,128)(2,1)} %param.6) | copy-start | bytes 24580
  33.0 257.0 %all-to-all-start = ((bf16[1,16,128,4096]{3,2,0,1:T(8,128)(2,1)}), bf16[1,16,128,4096]{3,2,0,1:T(8,128)(2,1)}, u32[]{:S(2)}, u32[]{:S(2)}) async-start(bf16[1,16,128,4096]{3,2,0,1:T(8,128)(2,1)} %bitcast_select_fusion), calls=%async_computation | async-start | bytes 33554432 | tf_op jit(solution)/shard_map/all_to_all | solution.py:31
  40.2 351.8 %all-reduce.2.cloned.1.call-start = ((), (), s32[]{:S(2)}) async-start(), calls=%async_computation.1 | async-start | bytes 8388608 | tf_op jit(solution)/shard_map/psum | solution.py:42
  52.2 5.8 %copy-start.2 = (bf16[1,64,64]{2,1,0:T(8,128)(2,1)S(1)}, bf16[1,64,64]{2,1,0:T(8,128)(2,1)}, u32[]{:S(2)}) copy-start(bf16[1,64,64]{2,1,0:T(8,128)(2,1)} %param.7) | copy-start | bytes 24580
  82.2 11.2 %copy-start.3 = (s32[64,2]{0,1:T(2,128)S(1)}, s32[64,2]{0,1:T(2,128)}, u32[]{:S(2)}) copy-start(s32[64,2]{0,1:T(2,128)} %param.9) | copy-start | bytes 1540
  289.9 103.9 %copy-start.1 = (bf16[1,64,64]{2,1,0:T(8,128)(2,1)S(1)}, bf16[1,64,64]{2,1,0:T(8,128)(2,1)}, u32[]{:S(2)}) copy-start(bf16[1,64,64]{2,1,0:T(8,128)(2,1)} %param.6) | copy-start | bytes 24580
Sparse Core Ops, SparseCore 0:
  320.3 71.6 all-reduce.1
where the time goes:
time: 402 us; the launch traced here: 401 us
  waiting for transfers between devices  268 us (67%)
  local copies, waits for them, and re-layouts  53 us (13%)
  matrix products  42.8 us (11%)
  other arithmetic  15.9 us (4%)
  between operations  13.4 us (3%)
  starting transfers between devices  7.28 us (2%)
    all_to_all x1, waiting for transfers between devices, on_device(): lax.all_to_all(outgoing, 'ex', split_axis=1, concat_axis=1, tiled=True)  197 us
    psum x1, waiting for transfers between devices, on_device(): total = lax.psum(terms, 'lay')  71.8 us
    dot_general x1, matrix products, on_device(): jnp.einsum('lqx,lmq->xm', left, right, preferred_element_type=jnp.float32)  24.1 us
    select_n x2, other arithmetic, on_device(): outgoing = jnp.take(blocks, wanted, axis=1)  15 us
    dot_general x1, matrix products, precondition(): jnp.einsum('lpo,loje->lpje', prec_out, inner, preferred_element_type=jnp....  12.9 us
    unnamed x9, local copies, waits for them, and re-layouts  12 us
    convert_element_type x1, local copies, waits for them, and re-layouts, precondition(): return outer.astype(jnp.bfloat16).reshape(layer_count, width, example_rows)  11.3 us
    dot_general x1, local copies, waits for them, and re-layouts, on_device(): jnp.einsum('lqx,lmq->xm', left, right, preferred_element_type=jnp.float32)  11.2 us
  transfers between devices with their start and end apart: 2, of which 2 were waited for; matrix products, arithmetic and copies ran while one was open for 13% of the time, Pallas kernels for 0%

commit v1 on v0

--- a/solution.py
+++ b/solution.py
@@ -39,7 +39,7 @@
     pair_count = pairs.shape[0]
     share = pair_count // lax.axis_size("lay")
     terms = pick_tiles(products, first, source)
-    total = lax.psum(terms, "lay")
+    total = jnp.sum(lax.all_gather(terms, "lay"), axis=0)
     return lax.dynamic_slice_in_dim(total, lax.axis_index("lay") * share, share, 0)
 
 

time: 402 us -> 501 us (1.25)
  waiting for transfers between devices: 268 us -> 352 us
  other arithmetic: 15.9 us -> 30.1 us
    all_gather x0 -> x1, waiting for transfers between devices: none -> 155 us  [on_device(): total = jnp.sum(lax.all_gather(terms, 'lay'), axis=0)]
    psum x1 -> x0, waiting for transfers between devices: 71.8 us -> none  [on_device(): total = lax.psum(terms, 'lay')]
    reduce_sum x0 -> x1, other arithmetic: none -> 14.2 us  [on_device(): total = jnp.sum(lax.all_gather(terms, 'lay'), axis=0)]
  transfers between devices with their start and end apart: 2 -> 2, of which waited for: 2 -> 2; matrix products, arithmetic and copies ran while one was open for 13% -> 11% of each run, Pallas kernels for 0% -> 0%
where the time goes in v1:
time: 501 us; the launch traced here: 498 us
  waiting for transfers between devices  352 us (70%)
  local copies, waits for them, and re-layouts  53.2 us (11%)
  matrix products  42.8 us (9%)
  other arithmetic  30.1 us (6%)
  between operations  13.4 us (3%)
  starting transfers between devices  7.26 us (1%)
    all_to_all x1, waiting for transfers between devices, on_device(): lax.all_to_all(outgoing, 'ex', split_axis=1, concat_axis=1, tiled=True)  197 us
    all_gather x1, waiting for transfers between devices, on_device(): total = jnp.sum(lax.all_gather(terms, 'lay'), axis=0)  155 us
    dot_general x1, matrix products, on_device(): jnp.einsum('lqx,lmq->xm', left, right, preferred_element_type=jnp.float32)  24.1 us
    select_n x2, other arithmetic, on_device(): outgoing = jnp.take(blocks, wanted, axis=1)  15 us
    reduce_sum x1, other arithmetic, on_device(): total = jnp.sum(lax.all_gather(terms, 'lay'), axis=0)  14.2 us
    dot_general x1, matrix products, precondition(): jnp.einsum('lpo,loje->lpje', prec_out, inner, preferred_element_type=jnp....  12.9 us
    unnamed x9, local copies, waits for them, and re-layouts  12 us
    convert_element_type x1, local copies, waits for them, and re-layouts, precondition(): return outer.astype(jnp.bfloat16).reshape(layer_count, width, example_rows)  11.3 us
  transfers between devices with their start and end apart: 2, of which 2 were waited for; matrix products, arithmetic and copies ran while one was open for 11% of the time, Pallas kernels for 0%

profile of v1, /device:TPU:0, one launch (start us, length us, event | category | flops | bytes accessed | tf_op | source)
XLA Modules:
  0.0 498.3 jit_solution(15924037794699853081)
XLA Ops:
  6.5 0.0 copy-start
  6.5 0.9 fusion.8
  7.4 0.9 and_reduce_fusion
  8.3 10.6 %gather_fusion = bf16[16,128,4096]{2,1,0:T(8,128)(2,1)} fusion(bf16[8,128,4096]{2,1,0:T(8,128)(2,1)} %bitcast.40, s32[1024]{0:T(1024)S(1)} %pad_clamp_fusion), kind=kCustom, calls=%fused_computation | custom fusion | bytes 33554496 | tf_op jit(solution)/shard_map/jit(_take)/gather | solution.py:30
  18.9 14.2 %bitcast_select_fusion = bf16[1,16,128,4096]{3,2,0,1:T(8,128)(2,1)} fusion(bf16[16,128,4096]{2,1,0:T(8,128)(2,1)} %gather_fusion, pred[16]{0:T(512)(128)(4,1)S(1)} %and_reduce_fusion), kind=kLoop, calls=%fused_computation.4 | loop fusion | flops 8388608 | bytes 33554448 | tf_op jit(solution)/shard_map/jit(_take)/select_n | solution.py:30
  33.1 7.2 %all-to-all-start = ((bf16[1,16,128,4096]{3,2,0,1:T(8,128)(2,1)}), bf16[1,16,128,4096]{3,2,0,1:T(8,128)(2,1)}, u32[]{:S(2)}, u32[]{:S(2)}) async-start(bf16[1,16,128,4096]{3,2,0,1:T(8,128)(2,1)} %bitcast_select_fusion), calls=%async_computation | async-start | bytes 33554432 | tf_op jit(solution)/shard_map/all_to_all | solution.py:31
  40.3 0.0 all-gather.3.cloned.1.call-start
  40.4 12.0 %copy.14 = bf16[1,1024,4096]{1,2,0:T(8,128)(2,1)} copy(bf16[1,1024,4096]{2,1,0:T(8,128)(2,1)} %param.5) | data formatting | bytes 16777216 | tf_op args[0]
  52.3 0.0 copy-done
  52.3 0.0 copy-start.2
  52.3 5.8 %convert_bitcast_fusion.1 = bf16[64,64,1024]{2,1,0:T(8,128)(2,1)S(1)} fusion(bf16[64,64,1024]{2,1,0:T(8,128)(2,1)} %bitcast.42, bf16[1,64,64]{2,1,0:T(8,128)(2,1)S(1)} %copy-done), kind=kOutput, calls=%fused_computation.8 | convolution fusion | flops 541065216 | bytes 16785408 | tf_op jit(solution)/shard_map/loie,lij->loje/dot_general | solution.py:13
  58.1 0.0 copy-done.2
  58.1 12.9 %convert_bitcast_fusion = bf16[64,64,1024]{2,0,1:T(8,128)(2,1)} fusion(bf16[64,64,1024]{2,1,0:T(8,128)(2,1)S(1)} %convert_bitcast_fusion.1, bf16[1,64,64]{2,1,0:T(8,128)(2,1)S(1)} %copy-done.2), kind=kOutput, calls=%fused_computation.7 | convolution fusion | flops 541065216 | bytes 16785408 | tf_op jit(solution)/shard_map/lpo,loje->lpje/dot_general | solution.py:16
  71.0 11.3 %copy.17 = bf16[64,64,1024]{2,1,0:T(8,128)(2,1)} copy(bf16[64,64,1024]{2,0,1:T(8,128)(2,1)} %convert_bitcast_fusion) | data formatting | bytes 16777216 | tf_op jit(solution)/shard_map/convert_element_type | solution.py:17
  82.3 0.0 copy-start.3
  82.3 11.2 %copy.22 = bf16[1024,4096]{1,0:T(8,128)(2,1)} copy(bf16[1024,4096]{0,1:T(8,128)(2,1)} %bitcast.43) | data formatting | bytes 16777216 | tf_op jit(solution)/shard_map/lqx,lmq->xm/dot_general | solution.py:35
  93.5 0.0 copy-done.3
  93.5 196.5 %all-to-all-done = bf16[1,16,128,4096]{3,2,0,1:T(8,128)(2,1)} async-done(((bf16[1,16,128,4096]{3,2,0,1:T(8,128)(2,1)}), bf16[1,16,128,4096]{3,2,0,1:T(8,128)(2,1)}, u32[]{:S(2)}, u32[]{:S(2)}) %all-to-all-start) | async-done | bytes 16777248 | tf_op jit(solution)/shard_map/all_to_all | solution.py:31
  290.0 24.1 %fusion = f32[8,128,16,128]{3,1,2,0:T(8,128)} fusion(bf16[8,128,4096,1]{2,1,3,0:T(8,128)(2,1)} %bitcast.44, bf16[1,16,128,4096]{3,2,0,1:T(8,128)(2,1)} %all-to-all-done), kind=kOutput, calls=%fused_computation.2 | convolution fusion | flops 17179869184 | bytes 33554432 | tf_op jit(solution)/shard_map/lqx,lmq->xm/dot_general | solution.py:35
  314.1 6.2 %gather_fusion.1 = f32[64,128,128]{2,1,0:T(8,128)} fusion(f32[8,128,16,128]{3,1,2,0:T(8,128)} %fusion, s32[64]{0:T(128)S(1)} %fusion.14), kind=kCustom, calls=%fused_computation.1 | custom fusion | bytes 8389120 | tf_op jit(solution)/shard_map/gather | solution.py:21
  320.4 0.0 all-gather.3.cloned.1.call-update
  320.4 155.0 %all-gather.3.cloned.1.call-done = f32[512,128,128]{2,1,0:T(8,128)} async-done(((f32[64,128,128]{2,1,0:T(8,128)}), f32[512,128,128]{2,1,0:T(8,128)}) %all-gather.3.cloned.1.call-update) | async-done | bytes 33554448 | tf_op jit(solution)/shard_map/all_gather | solution.py:42
  475.4 0.0 copy-start.1
  475.4 14.2 %reduce_sum.9 = f32[64,128,128]{2,1,0:T(8,128)} reduce(f32[8,64,128,128]{3,2,1,0:T(8,128)} %bitcast.41, f32[]{:T(128)} %constant.36.clone.1), dimensions={0}, to_apply=%region_0.1 | reduce | flops 7340032 | bytes 37748740 | tf_op jit(solution)/shard_map/reduce_sum | solution.py:42
  489.6 1.9 constant_dynamic-slice_fusion
  491.4 0.0 copy-done.1
  (2 shorter events, 0.0 us)
Async XLA Ops:
  6.5 45.8 %copy-start = (bf16[1,64,64]{2,1,0:T(8,128)(2,1)S(1)}, bf16[1,64,64]{2,1,0:T(8,128)(2,1)}, u32[]{:S(2)}) copy-start(bf16[1,64,64]{2,1,0:T(8,128)(2,1)} %param.6) | copy-start | bytes 24580
  33.1 256.9 %all-to-all-start = ((bf16[1,16,128,4096]{3,2,0,1:T(8,128)(2,1)}), bf16[1,16,128,4096]{3,2,0,1:T(8,128)(2,1)}, u32[]{:S(2)}, u32[]{:S(2)}) async-start(bf16[1,16,128,4096]{3,2,0,1:T(8,128)(2,1)} %bitcast_select_fusion), calls=%async_computation | async-start | bytes 33554432 | tf_op jit(solution)/shard_map/all_to_all | solution.py:31
  40.3 435.1 %all-gather.3.cloned.1.call-start = ((), (), s32[]{:S(2)}) async-start(), calls=%async_computation.1 | async-start | bytes 37748736 | tf_op jit(solution)/shard_map/all_gather | solution.py:42
  52.3 5.8 %copy-start.2 = (bf16[1,64,64]{2,1,0:T(8,128)(2,1)S(1)}, bf16[1,64,64]{2,1,0:T(8,128)(2,1)}, u32[]{:S(2)}) copy-start(bf16[1,64,64]{2,1,0:T(8,128)(2,1)} %param.7) | copy-start | bytes 24580
  82.3 11.2 %copy-start.3 = (s32[64,2]{0,1:T(2,128)S(1)}, s32[64,2]{0,1:T(2,128)}, u32[]{:S(2)}) copy-start(s32[64,2]{0,1:T(2,128)} %param.9) | copy-start | bytes 1540
  475.4 16.0 %copy-start.1 = (bf16[1,64,64]{2,1,0:T(8,128)(2,1)S(1)}, bf16[1,64,64]{2,1,0:T(8,128)(2,1)}, u32[]{:S(2)}) copy-start(bf16[1,64,64]{2,1,0:T(8,128)(2,1)} %param.6) | copy-start | bytes 24580
Sparse Core Ops, SparseCore 0:
  320.5 154.8 all-gather.2
